TPU v7x, 512 devices: a whole 4x8x8 slice. The times are simulated.
512 devices in a mesh: row: 8 (over z), col: 16 (over y, core), depth: 4 (over x).
Axes of the slice: x: 4, y: 8, z: 8, core: 2. Of those that a mesh axis runs over, the one named last changes fastest.
Arguments:
- tokens: bfloat16 [4096, 8192], P(('row', 'col'), 'depth'), may hold values from -6 to 6
- gate_weight: bfloat16 [8192, 14336], P(('depth', 'row'), 'col'), may hold values from -0.0625 to 0.0625
- up_weight: bfloat16 [8192, 14336], P(('depth', 'row'), 'col'), may hold values from -0.0625 to 0.0625
- down_weight: bfloat16 [14336, 8192], P(('col', 'row'), 'depth'), may hold values from -0.125 to 0.125
- gate_keep: int32 [64, 112], replicated, may hold values from 0 to 1, as said below
- up_keep: int32 [64, 112], replicated, may hold values from 0 to 1, as said below
- down_keep: int32 [112, 64], replicated, may hold values from 0 to 1, as said below
Outputs:
- mixed: bfloat16 [4096, 8192], P(('row', 'col'), 'depth')
Inputs may be any that keep to these rules, and one draw needn't show every extreme that they name: `gate_keep`: 1 marks a kept block of the gate projection, 0 a dropped one. `up_keep`: 1 marks a kept block of the up projection, 0 a dropped one. `down_keep`: 1 marks a kept block of the down projection, 0 a dropped one.
All inputs are finite; a program needn't handle non-finite values.
Results may differ from a plain program's by a relative error of at most 0.005.
Values may be sent and summed in bfloat16 or wider, within the bound.
No kernel may reach another device: no remote copies, remote signals or barrier semaphores. Data moves between devices by JAX's collectives and lax.ppermute only.
A program may use at most 64 MiB of HBM per device.

v0:
```python
import jax
import jax.numpy as jnp
from jax import lax
from jax.sharding import PartitionSpec as P

BLOCK = 128


def keep_table(keep, row_start, col_start, row_count, col_count):
    keep_bits = keep.astype(jnp.bfloat16)
    row_ids = (row_start + jnp.arange(row_count, dtype=jnp.int32)) // BLOCK
    col_ids = (col_start + jnp.arange(col_count, dtype=jnp.int32)) // BLOCK
    pick_rows = (row_ids[:, None] == jnp.arange(keep.shape[0], dtype=jnp.int32)[None, :]).astype(
        jnp.bfloat16
    )
    pick_cols = (jnp.arange(keep.shape[1], dtype=jnp.int32)[:, None] == col_ids[None, :]).astype(
        jnp.bfloat16
    )
    inner = jnp.dot(keep_bits, pick_cols, preferred_element_type=jnp.float32).astype(jnp.bfloat16)
    return jnp.dot(pick_rows, inner, preferred_element_type=jnp.float32).astype(jnp.bfloat16)


def add_panel(token_block, piece):
    return jnp.dot(token_block, piece, preferred_element_type=jnp.float32)


def on_device(tokens, gate_weight, up_weight, down_weight, gate_keep, up_keep, down_keep):
    depth_pos = lax.axis_index("depth")
    row_pos = lax.axis_index("row")
    column_pos = lax.axis_index("col")
    row_total = lax.axis_size("row")
    feature_rows = gate_weight.shape[0]
    hidden_cols = gate_weight.shape[1]
    feature_start = (depth_pos * row_total + row_pos) * feature_rows
    hidden_start = column_pos * hidden_cols
    gate_masked = gate_weight * keep_table(
        gate_keep, feature_start, hidden_start, feature_rows, hidden_cols
    )
    up_masked = up_weight * keep_table(
        up_keep, feature_start, hidden_start, feature_rows, hidden_cols
    )
    down_rows_count = down_weight.shape[0]
    down_features = down_weight.shape[1]
    down_start = (column_pos * row_total + row_pos) * down_rows_count
    down_masked = down_weight * keep_table(
        down_keep, down_start, depth_pos * down_features, down_rows_count, down_features
    )
    token_block = lax.all_gather(tokens, "col", axis=0, tiled=True)

    def add_one(piece):
        return add_panel(token_block, piece)

    gate = add_one(lax.all_gather(gate_masked, "row", axis=0, tiled=True))
    up = add_one(lax.all_gather(up_masked, "row", axis=0, tiled=True))
    both = jnp.stack((gate, up), 0)
    total = lax.psum(both, "depth")
    hidden = (jax.nn.silu(total[0]) * total[1]).astype(jnp.bfloat16)
    down_block = lax.all_gather(down_masked, "row", axis=0, tiled=True)
    mixed = lax.psum_scatter(
        jnp.dot(hidden, down_block, preferred_element_type=jnp.float32),
        "col",
        scatter_dimension=0,
        tiled=True,
    )
    return mixed.astype(jnp.bfloat16)


def solution(mesh):
    placed = (
        P(("row", "col"), "depth"),
        P(("depth", "row"), "col"),
        P(("depth", "row"), "col"),
        P(("col", "row"), "depth"),
        P(),
        P(),
        P(),
    )
    return jax.shard_map(
        on_device, mesh=mesh, in_specs=placed, out_specs=P(("row", "col"), "depth"), check_vma=False
    )
```

profile of v0, /device:TPU:25, one launch (start us, length us, event | category | flops | bytes accessed | tf_op | source)
XLA Modules:
  0.0 393.9 jit_solution(8674119538249657588)
XLA Ops:
  6.5 0.0 copy-start
  6.5 0.0 copy-start.1
  6.5 0.0 all-gather.7.cloned.1.call-start
  6.5 0.7 all-gather.7.cloned.1.call-update
  7.3 0.0 all-gather.9.cloned.1.call-start
  7.4 2.3 fusion.4
  9.7 0.0 all-gather.9.cloned.1.call-update
  9.7 0.0 all-gather.5.cloned.1.call-start
  9.8 2.3 fusion.3
  12.1 0.0 all-gather.5.cloned.1.call-update
  12.1 0.0 all-gather.11.cloned.1.call-start
  12.2 0.0 copy-done
  12.2 0.0 copy-done.1
  12.2 1.4 fusion
  13.7 0.0 all-gather.11.cloned.1.call-update
  13.7 0.0 all-reduce.2.cloned.1.call-start
  13.7 42.2 %all-gather.7.cloned.1.call-done = bf16[512,2048]{1,0:T(8,128)(2,1)} async-done(((bf16[32,2048]{1,0:T(8,128)(2,1)}), bf16[512,2048]{1,0:T(8,128)(2,1)}) %all-gather.7.cloned.1.call-update) | async-done | bytes 2097168 | tf_op jit(solution)/shard_map/all_gather | solution.py:48
  55.9 54.2 %all-gather.9.cloned.1.call-done = bf16[2048,896]{1,0:T(8,128)(2,1)} async-done(((bf16[256,896]{1,0:T(8,128)(2,1)}), bf16[2048,896]{1,0:T(8,128)(2,1)}) %all-gather.9.cloned.1.call-update) | async-done | bytes 3670032 | tf_op jit(solution)/shard_map/all_gather | solution.py:54
  110.2 4.8 %convolution_bitcast_fusion = f32[1,512,896]{1,2,0:T(8,128)S(1)} fusion(bf16[2048,896]{1,0:T(8,128)(2,1)} %all-gather.9.cloned.1.call-done, bf16[512,2048]{1,0:T(8,128)(2,1)} %all-gather.7.cloned.1.call-done), kind=kOutput, calls=%fused_computation.8 | convolution fusion | flops 1879048192 | bytes 7602176 | tf_op jit(solution)/shard_map/dot_general | solution.py:24
  115.0 48.7 %all-gather.5.cloned.1.call-done = bf16[2048,896]{1,0:T(8,128)(2,1)} async-done(((bf16[256,896]{1,0:T(8,128)(2,1)}), bf16[2048,896]{1,0:T(8,128)(2,1)}) %all-gather.5.cloned.1.call-update) | async-done | bytes 3670032 | tf_op jit(solution)/shard_map/all_gather | solution.py:53
  163.7 4.8 %convolution_bitcast_fusion.1 = f32[1,512,896]{1,2,0:T(8,128)S(1)} fusion(bf16[2048,896]{1,0:T(8,128)(2,1)} %all-gather.5.cloned.1.call-done, bf16[512,2048]{1,0:T(8,128)(2,1)} %all-gather.7.cloned.1.call-done), kind=kOutput, calls=%fused_computation.9 | convolution fusion | flops 1879048192 | bytes 7602176 | tf_op jit(solution)/shard_map/dot_general | solution.py:24
  168.5 2.3 pad_maximum_fusion
  170.8 0.0 all-reduce.2.cloned.1.call-update
  170.9 0.0 reduce-scatter.2.cloned.1.call-start
  170.9 46.2 %all-gather.11.cloned.1.call-done = bf16[896,2048]{1,0:T(8,128)(2,1)} async-done(((bf16[112,2048]{1,0:T(8,128)(2,1)}), bf16[896,2048]{1,0:T(8,128)(2,1)}) %all-gather.11.cloned.1.call-update) | async-done | bytes 3670032 | tf_op jit(solution)/shard_map/all_gather | solution.py:58
  217.1 95.3 %all-reduce.2.cloned.1.call-done = f32[2,512,896]{1,2,0:T(8,128)} async-done(((f32[2,512,896]{1,2,0:T(8,128)}), f32[2,512,896]{1,2,0:T(8,128)}) %all-reduce.2.cloned.1.call-update) | async-done | bytes 3670032 | tf_op jit(solution)/shard_map/psum | solution.py:56
  312.4 7.7 %fusion.5 = f32[512,2048]{1,0:T(8,128)} fusion(bf16[896,2048]{1,0:T(8,128)(2,1)} %all-gather.11.cloned.1.call-done, f32[2,512,896]{1,2,0:T(8,128)} %all-reduce.2.cloned.1.call-done), kind=kOutput, calls=%fused_computation.16 | convolution fusion | flops 1881800704 | bytes 11534336 | tf_op jit(solution)/shard_map/dot_general | solution.py:60
  320.0 0.0 reduce-scatter.2.cloned.1.call-update
  320.1 65.3 %reduce-scatter.2.cloned.1.call-done = f32[32,2048]{1,0:T(8,128)} async-done(((f32[512,2048]{1,0:T(8,128)}), f32[32,2048]{1,0:T(8,128)}) %reduce-scatter.2.cloned.1.call-update) | async-done | bytes 262160 | tf_op jit(solution)/shard_map/reduce_scatter | solution.py:59
  385.4 1.6 convert_element_type.52
  (4 shorter events, 0.0 us)
Async XLA Ops:
  6.5 5.7 %copy-start = (bf16[112,2048]{1,0:T(8,128)(2,1)S(1)}, bf16[112,2048]{1,0:T(8,128)(2,1)}, u32[]{:S(2)}) copy-start(bf16[112,2048]{1,0:T(8,128)(2,1)} %param.10) | copy-start | bytes 1376260
  6.5 5.7 %copy-start.1 = (s32[112,64]{0,1:T(8,128)S(1)}, s32[112,64]{0,1:T(8,128)}, u32[]{:S(2)}) copy-start(s32[112,64]{0,1:T(8,128)} %param.13) | copy-start | bytes 86020
  6.5 49.4 %all-gather.7.cloned.1.call-start = ((), (), s32[]{:S(2)}) async-start(), calls=%async_computation.2 | async-start | bytes 2228224 | tf_op jit(solution)/shard_map/all_gather | solution.py:48
  7.3 102.9 %all-gather.9.cloned.1.call-start = ((), (), s32[]{:S(2)}) async-start(), calls=%async_computation.3 | async-start | bytes 4128768 | tf_op jit(solution)/shard_map/all_gather | solution.py:54
  9.7 154.0 %all-gather.5.cloned.1.call-start = ((), (), s32[]{:S(2)}) async-start(), calls=%async_computation.1 | async-start | bytes 4128768 | tf_op jit(solution)/shard_map/all_gather | solution.py:53
  12.1 205.0 %all-gather.11.cloned.1.call-start = ((), (), s32[]{:S(2)}) async-start(), calls=%async_computation.5 | async-start | bytes 4128768 | tf_op jit(solution)/shard_map/all_gather | solution.py:58
  13.7 298.7 %all-reduce.2.cloned.1.call-start = ((), (), s32[]{:S(2)}) async-start(), calls=%async_computation.4 | async-start | bytes 7340032 | tf_op jit(solution)/shard_map/psum | solution.py:56
  170.9 214.5 %reduce-scatter.2.cloned.1.call-start = ((), (), s32[]{:S(2)}) async-start(), calls=%async_computation.6 | async-start | bytes 4456448 | tf_op jit(solution)/shard_map/reduce_scatter | solution.py:59
Sparse Core Ops, SparseCore 0:
  9.5 46.3 all-gather.6
  58.0 52.1 all-gather.8
  112.2 51.4 all-gather.4
  165.6 51.3 all-gather.10
  219.3 93.0 all-reduce.1
  320.2 65.1 reduce-scatter.1
where the time goes:
time: 394 us
  waiting for transfers between devices  353 us (90%)
  matrix products  23.4 us (6%)
  between operations  13.5 us (3%)
  other arithmetic  4 us (1%)
    psum x1, waiting for transfers between devices, on_device(): total = lax.psum(both, 'depth')  95.3 us
    reduce_scatter x1, waiting for transfers between devices, on_device(): lax.psum_scatter(jnp.dot(hidden, down_block, preferred_element_type=jnp.f...  65.3 us
    all_gather x1, waiting for transfers between devices, on_device(): up = add_one(lax.all_gather(up_masked, 'row', axis=0, tiled=True))  54.2 us
    all_gather x1, waiting for transfers between devices, on_device(): gate = add_one(lax.all_gather(gate_masked, 'row', axis=0, tiled=True))  48.7 us
    all_gather x1, waiting for transfers between devices, on_device(): down_block = lax.all_gather(down_masked, 'row', axis=0, tiled=True)  46.2 us
    all_gather x1, waiting for transfers between devices, on_device(): token_block = lax.all_gather(tokens, 'col', axis=0, tiled=True)  42.2 us
    dot_general x2, matrix products, add_panel(): return jnp.dot(token_block, piece, preferred_element_type=jnp.float32)  9.61 us
  transfers between devices with their start and end apart: 6, of which 6 were waited for; matrix products, arithmetic and copies ran while one was open for 5% of the time, Pallas kernels for 0%

commit v1 on v0

--- a/solution.py
+++ b/solution.py
@@ -45,7 +45,9 @@
     down_masked = down_weight * keep_table(
         down_keep, down_start, depth_pos * down_features, down_rows_count, down_features
     )
-    token_block = lax.all_gather(tokens, "col", axis=0, tiled=True)
+    token_block = jnp.concatenate(
+        lax.all_to_all(jnp.stack([tokens] * lax.axis_size("col")), "col", 0, 0), axis=0
+    )
 
     def add_one(piece):
         return add_panel(token_block, piece)

time: 394 us -> 351 us (0.89)
  the two profiles are of different devices: /device:TPU:25 before, /device:TPU:31 now
where the time goes in v1:
time: 351 us
  waiting for transfers between devices  254 us (72%)
  blocking collectives  56.1 us (16%)
  matrix products  23.5 us (7%)
  between operations  13.2 us (4%)
  other arithmetic  3.95 us (1%)
    psum x1, waiting for transfers between devices, on_device(): total = lax.psum(both, 'depth')  93.5 us
    reduce_scatter x1, waiting for transfers between devices, on_device(): lax.psum_scatter(jnp.dot(hidden, down_block, preferred_element_type=jnp.f...  67.4 us
    all_to_all x1, blocking collectives, on_device(): lax.all_to_all(jnp.stack([tokens] * lax.axis_size('col')), 'col', 0, 0)  56.1 us
    all_gather x1, waiting for transfers between devices, on_device(): down_block = lax.all_gather(down_masked, 'row', axis=0, tiled=True)  46.9 us
    all_gather x1, waiting for transfers between devices, on_device(): gate = add_one(lax.all_gather(gate_masked, 'row', axis=0, tiled=True))  45.7 us
    dot_general x2, matrix products, add_panel(): return jnp.dot(token_block, piece, preferred_element_type=jnp.float32)  9.76 us
    dot_general x1, matrix products, on_device(): jnp.dot(hidden, down_block, preferred_element_type=jnp.float32)  7.61 us
  transfers between devices with their start and end apart: 5, of which 4 were waited for; matrix products, arithmetic and copies ran while one was open for 5% of the time, Pallas kernels for 0%

profile of v1, /device:TPU:31, one launch (start us, length us, event | category | flops | bytes accessed | tf_op | source)
XLA Modules:
  0.0 350.8 jit_solution(8787106681206974614)
XLA Ops:
  6.5 0.0 copy-start.1
  6.5 0.0 copy-start.3
  6.5 0.0 all-gather.6.cloned.1.call-start
  6.6 0.0 copy-start.2
  6.6 2.4 fusion.4
  9.0 0.0 all-gather.6.cloned.1.call-update
  9.0 0.0 all-gather.4.cloned.1.call-start
  9.1 2.3 fusion.3
  11.4 0.0 all-gather.4.cloned.1.call-update
  11.4 0.0 all-gather.8.cloned.1.call-start
  11.5 0.0 copy-done.1
  11.5 0.0 copy-done.3
  11.5 1.4 fusion
  13.0 0.0 all-gather.8.cloned.1.call-update
  13.0 0.0 all-reduce.2.cloned.1.call-start
  13.0 0.0 copy-done.2
  13.1 0.2 stack.8
  13.3 56.1 %all_to_all.5 = bf16[16,32,2048]{2,1,0:T(8,128)(2,1)S(1)} all-to-all(bf16[16,32,2048]{2,1,0:T(8,128)(2,1)S(1)} %stack.8), channel_id=1, replica_groups=mesh['row'=8,'col'=16,'depth'=4] {'col'}, dimensions={0} | all-to-all | bytes 4194304 | tf_op jit(solution)/shard_map/all_to_all | solution.py:49
  69.4 0.0 all-gather.6.cloned.1.call-done
  69.4 5.5 %convolution_bitcast_fusion = f32[1,512,896]{1,2,0:T(8,128)} fusion(bf16[2048,896]{1,0:T(8,128)(2,1)} %all-gather.6.cloned.1.call-done, bf16[512,2048]{1,0:T(8,128)(2,1)S(1)} %bitcast.26), kind=kOutput, calls=%fused_computation.8 | convolution fusion | flops 1879048192 | bytes 7602176 | tf_op jit(solution)/shard_map/dot_general | solution.py:24
  74.9 45.7 %all-gather.4.cloned.1.call-done = bf16[2048,896]{1,0:T(8,128)(2,1)} async-done(((bf16[256,896]{1,0:T(8,128)(2,1)}), bf16[2048,896]{1,0:T(8,128)(2,1)}) %all-gather.4.cloned.1.call-update) | async-done | bytes 3670032 | tf_op jit(solution)/shard_map/all_gather | solution.py:55
  120.7 0.0 copy-start
  120.7 4.3 %convolution_bitcast_fusion.1 = f32[1,512,896]{1,2,0:T(8,128)S(1)} fusion(bf16[2048,896]{1,0:T(8,128)(2,1)} %all-gather.4.cloned.1.call-done, bf16[512,2048]{1,0:T(8,128)(2,1)S(1)} %bitcast.27), kind=kOutput, calls=%fused_computation.9 | convolution fusion | flops 1879048192 | bytes 7602176 | tf_op jit(solution)/shard_map/dot_general | solution.py:24
  124.9 0.0 copy-done
  124.9 2.3 pad_maximum_fusion
  127.2 0.0 all-reduce.2.cloned.1.call-update
  127.3 0.0 reduce-scatter.2.cloned.1.call-start
  127.3 46.9 %all-gather.8.cloned.1.call-done = bf16[896,2048]{1,0:T(8,128)(2,1)} async-done(((bf16[112,2048]{1,0:T(8,128)(2,1)}), bf16[896,2048]{1,0:T(8,128)(2,1)}) %all-gather.8.cloned.1.call-update) | async-done | bytes 3670032 | tf_op jit(solution)/shard_map/all_gather | solution.py:60
  174.2 93.5 %all-reduce.2.cloned.1.call-done = f32[2,512,896]{1,2,0:T(8,128)} async-done(((f32[2,512,896]{1,2,0:T(8,128)}), f32[2,512,896]{1,2,0:T(8,128)}) %all-reduce.2.cloned.1.call-update) | async-done | bytes 3670032 | tf_op jit(solution)/shard_map/psum | solution.py:58
  267.7 7.6 %fusion.5 = f32[512,2048]{1,0:T(8,128)} fusion(bf16[896,2048]{1,0:T(8,128)(2,1)} %all-gather.8.cloned.1.call-done, f32[2,512,896]{1,2,0:T(8,128)} %all-reduce.2.cloned.1.call-done), kind=kOutput, calls=%fused_computation.16 | convolution fusion | flops 1881800704 | bytes 11534336 | tf_op jit(solution)/shard_map/dot_general | solution.py:62
  275.3 0.0 reduce-scatter.2.cloned.1.call-update
  275.3 67.4 %reduce-scatter.2.cloned.1.call-done = f32[32,2048]{1,0:T(8,128)} async-done(((f32[512,2048]{1,0:T(8,128)}), f32[32,2048]{1,0:T(8,128)}) %reduce-scatter.2.cloned.1.call-update) | async-done | bytes 262160 | tf_op jit(solution)/shard_map/reduce_scatter | solution.py:61
  342.6 1.6 convert_element_type.52
  (4 shorter events, 0.0 us)
Async XLA Ops:
  6.5 5.0 %copy-start.1 = (bf16[112,2048]{1,0:T(8,128)(2,1)S(1)}, bf16[112,2048]{1,0:T(8,128)(2,1)}, u32[]{:S(2)}) copy-start(bf16[112,2048]{1,0:T(8,128)(2,1)} %param.10) | copy-start | bytes 1376260
  6.5 5.0 %copy-start.3 = (s32[112,64]{0,1:T(8,128)S(1)}, s32[112,64]{0,1:T(8,128)}, u32[]{:S(2)}) copy-start(s32[112,64]{0,1:T(8,128)} %param.13) | copy-start | bytes 86020
  6.5 62.9 %all-gather.6.cloned.1.call-start = ((), (), s32[]{:S(2)}) async-start(), calls=%async_computation.3 | async-start | bytes 4128768 | tf_op jit(solution)/shard_map/all_gather | solution.py:56
  6.6 6.5 %copy-start.2 = (bf16[32,2048]{1,0:T(8,128)(2,1)S(1)}, bf16[32,2048]{1,0:T(8,128)(2,1)}, u32[]{:S(2)}) copy-start(bf16[32,2048]{1,0:T(8,128)(2,1)} %param.7) | copy-start | bytes 393220
  9.0 111.6 %all-gather.4.cloned.1.call-start = ((), (), s32[]{:S(2)}) async-start(), calls=%async_computation.2 | async-start | bytes 4128768 | tf_op jit(solution)/shard_map/all_gather | solution.py:55
  11.4 162.8 %all-gather.8.cloned.1.call-start = ((), (), s32[]{:S(2)}) async-start(), calls=%async_computation.5 | async-start | bytes 4128768 | tf_op jit(solution)/shard_map/all_gather | solution.py:60
  13.0 254.7 %all-reduce.2.cloned.1.call-start = ((), (), s32[]{:S(2)}) async-start(), calls=%async_computation.4 | async-start | bytes 7340032 | tf_op jit(solution)/shard_map/psum | solution.py:58
  120.7 4.3 %copy-start = (f32[1,512,896]{1,2,0:T(8,128)S(1)}, f32[1,512,896]{1,2,0:T(8,128)}, u32[]{:S(2)}) copy-start(f32[1,512,896]{1,2,0:T(8,128)} %convolution_bitcast_fusion) | copy-start | bytes 5505028
  127.3 215.4 %reduce-scatter.2.cloned.1.call-start = ((), (), s32[]{:S(2)}) async-start(), calls=%async_computation.6 | async-start | bytes 4456448 | tf_op jit(solution)/shard_map/reduce_scatter | solution.py:61
Sparse Core Ops, SparseCore 0:
  9.4 57.6 all-gather.5
  69.2 51.3 all-gather.3
  122.7 51.3 all-gather.7
  176.4 91.2 all-reduce.1
  275.4 67.1 reduce-scatter.1

commit v2 on v0

--- a/solution.py
+++ b/solution.py
@@ -53,7 +53,9 @@
     gate = add_one(lax.all_gather(gate_masked, "row", axis=0, tiled=True))
     up = add_one(lax.all_gather(up_masked, "row", axis=0, tiled=True))
     both = jnp.stack((gate, up), 0)
-    total = lax.psum(both, "depth")
+    total = both
+    for hop in (1, 2):
+        total = total + lax.ppermute(total, "depth", [(dev, dev ^ hop) for dev in range(4)])
     hidden = (jax.nn.silu(total[0]) * total[1]).astype(jnp.bfloat16)
     down_block = lax.all_gather(down_masked, "row", axis=0, tiled=True)
     mixed = lax.psum_scatter(

time: 394 us -> 426 us (1.081)
  the two profiles are of different devices: /device:TPU:25 before, /device:TPU:31 now
where the time goes in v2:
time: 426 us
  waiting for transfers between devices  371 us (87%)
  matrix products  23.3 us (5%)
  between operations  13.3 us (3%)
  other arithmetic  12.8 us (3%)
  starting transfers between devices  5.9 us (1%)
    ppermute x2, waiting for transfers between devices, on_device(): lax.ppermute(total, 'depth', [(dev, dev ^ hop) for dev in range(4)])  158 us
    reduce_scatter x1, waiting for transfers between devices, on_device(): lax.psum_scatter(jnp.dot(hidden, down_block, preferred_element_type=jnp.f...  65.5 us
    all_gather x1, waiting for transfers between devices, on_device(): up = add_one(lax.all_gather(up_masked, 'row', axis=0, tiled=True))  54.2 us
    all_gather x1, waiting for transfers between devices, on_device(): gate = add_one(lax.all_gather(gate_masked, 'row', axis=0, tiled=True))  48.7 us
    all_gather x1, waiting for transfers between devices, on_device(): token_block = lax.all_gather(tokens, 'col', axis=0, tiled=True)  43.7 us
    dot_general x2, matrix products, add_panel(): return jnp.dot(token_block, piece, preferred_element_type=jnp.float32)  9.61 us
    add x2, other arithmetic, on_device(): total + lax.ppermute(total, 'depth', [(dev, dev ^ hop) for dev in range(4)])  8.79 us
  transfers between devices with their start and end apart: 7, of which 6 were waited for; matrix products, arithmetic and copies ran while one was open for 5% of the time, Pallas kernels for 0%

profile of v2, /device:TPU:31, one launch (start us, length us, event | category | flops | bytes accessed | tf_op | source)
XLA Modules:
  0.0 426.0 jit_solution(1652279846744225317)
XLA Ops:
  6.5 0.0 all-gather.7.cloned.1.call-start
  6.5 0.7 all-gather.7.cloned.1.call-update
  7.3 0.0 all-gather.9.cloned.1.call-start
  7.3 2.3 fusion.4
  9.7 0.0 all-gather.9.cloned.1.call-update
  9.7 0.0 all-gather.5.cloned.1.call-start
  9.8 2.3 fusion.3
  12.1 0.0 all-gather.5.cloned.1.call-update
  12.1 0.0 all-gather.11.cloned.1.call-start
  12.2 43.7 %all-gather.7.cloned.1.call-done = bf16[512,2048]{1,0:T(8,128)(2,1)} async-done(((bf16[32,2048]{1,0:T(8,128)(2,1)}), bf16[512,2048]{1,0:T(8,128)(2,1)}) %all-gather.7.cloned.1.call-update) | async-done | bytes 2097168 | tf_op jit(solution)/shard_map/all_gather | solution.py:48
  55.9 54.2 %all-gather.9.cloned.1.call-done = bf16[2048,896]{1,0:T(8,128)(2,1)} async-done(((bf16[256,896]{1,0:T(8,128)(2,1)}), bf16[2048,896]{1,0:T(8,128)(2,1)}) %all-gather.9.cloned.1.call-update) | async-done | bytes 3670032 | tf_op jit(solution)/shard_map/all_gather | solution.py:54
  110.1 4.8 %convolution_bitcast_fusion = f32[1,512,896]{1,2,0:T(8,128)S(1)} fusion(bf16[2048,896]{1,0:T(8,128)(2,1)} %all-gather.9.cloned.1.call-done, bf16[512,2048]{1,0:T(8,128)(2,1)} %all-gather.7.cloned.1.call-done), kind=kOutput, calls=%fused_computation.8 | convolution fusion | flops 1879048192 | bytes 7602176 | tf_op jit(solution)/shard_map/dot_general | solution.py:24
  114.9 48.7 %all-gather.5.cloned.1.call-done = bf16[2048,896]{1,0:T(8,128)(2,1)} async-done(((bf16[256,896]{1,0:T(8,128)(2,1)}), bf16[2048,896]{1,0:T(8,128)(2,1)}) %all-gather.5.cloned.1.call-update) | async-done | bytes 3670032 | tf_op jit(solution)/shard_map/all_gather | solution.py:53
  163.6 4.8 %convolution_bitcast_fusion.1 = f32[1,512,896]{1,2,0:T(8,128)S(1)} fusion(bf16[2048,896]{1,0:T(8,128)(2,1)} %all-gather.5.cloned.1.call-done, bf16[512,2048]{1,0:T(8,128)(2,1)} %all-gather.7.cloned.1.call-done), kind=kOutput, calls=%fused_computation.9 | convolution fusion | flops 1879048192 | bytes 7602176 | tf_op jit(solution)/shard_map/dot_general | solution.py:24
  168.4 0.0 copy-start
  168.4 0.0 copy-start.2
  168.5 0.0 copy-start.3
  168.5 2.3 pad_maximum_fusion
  170.8 0.2 copy-done
  170.9 2.5 collective-permute-start
  173.5 0.0 copy-done.2
  173.5 0.0 copy-done.3
  173.5 1.5 fusion
  175.0 0.0 all-gather.11.cloned.1.call-update
  175.0 0.0 reduce-scatter.2.cloned.1.call-start
  175.0 0.0 copy-start.1
  175.0 78.3 %collective-permute-done = f32[2,512,896]{1,2,0:T(8,128)} collective-permute-done((f32[2,512,896]{1,2,0:T(8,128)}, f32[2,512,896]{1,2,0:T(8,128)}, u32[]{:S(2)}, u32[]{:S(2)}) %collective-permute-start) | collective-permute-done | bytes 3670048 | tf_op jit(solution)/shard_map/ppermute | solution.py:58
  253.3 3.5 fusion.35
  256.8 3.3 collective-permute-start.1
  260.1 79.4 %collective-permute-done.1 = f32[2,512,896]{1,2,0:T(8,128)S(1)} collective-permute-done((f32[2,512,896]{1,2,0:T(8,128)S(1)}, f32[2,512,896]{1,2,0:T(8,128)S(1)}, u32[]{:S(2)}, u32[]{:S(2)}) %collective-permute-start.1) | collective-permute-done | bytes 3670048 | tf_op jit(solution)/shard_map/ppermute | solution.py:58
  339.5 0.0 copy-done.1
  339.5 5.3 %fusion.41 = f32[2,512,896]{1,2,0:T(8,128)} fusion(f32[2,512,896]{1,2,0:T(8,128)S(1)} %collective-permute-done.1, f32[2,512,896]{1,2,0:T(8,128)} %collective-permute-done, f32[1,512,896]{1,2,0:T(8,128)S(1)} %convolution_bitcast_fusion, f32[1,512,896]{1,2,0:T(8,128)S(1)} %copy-done.1), kind=kLoop, calls=%fused_computation.60 | loop fusion | flops 2752512 | bytes 14680064 | tf_op jit(solution)/shard_map/add | solution.py:58
  344.8 0.0 all-gather.11.cloned.1.call-done
  344.8 7.5 %fusion.5 = f32[512,2048]{1,0:T(8,128)} fusion(bf16[896,2048]{1,0:T(8,128)(2,1)} %all-gather.11.cloned.1.call-done, f32[2,512,896]{1,2,0:T(8,128)} %fusion.41), kind=kOutput, calls=%fused_computation.16 | convolution fusion | flops 1881800704 | bytes 11534336 | tf_op jit(solution)/shard_map/dot_general | solution.py:62
  352.4 0.0 reduce-scatter.2.cloned.1.call-update
  352.4 65.5 %reduce-scatter.2.cloned.1.call-done = f32[32,2048]{1,0:T(8,128)} async-done(((f32[512,2048]{1,0:T(8,128)}), f32[32,2048]{1,0:T(8,128)}) %reduce-scatter.2.cloned.1.call-update) | async-done | bytes 262160 | tf_op jit(solution)/shard_map/reduce_scatter | solution.py:61
  417.9 1.6 convert_element_type.52
  (4 shorter events, 0.0 us)
Async XLA Ops:
  6.5 49.3 %all-gather.7.cloned.1.call-start = ((), (), s32[]{:S(2)}) async-start(), calls=%async_computation.2 | async-start | bytes 2228224 | tf_op jit(solution)/shard_map/all_gather | solution.py:48
  7.3 102.8 %all-gather.9.cloned.1.call-start = ((), (), s32[]{:S(2)}) async-start(), calls=%async_computation.3 | async-start | bytes 4128768 | tf_op jit(solution)/shard_map/all_gather | solution.py:54
  9.7 153.9 %all-gather.5.cloned.1.call-start = ((), (), s32[]{:S(2)}) async-start(), calls=%async_computation.1 | async-start | bytes 4128768 | tf_op jit(solution)/shard_map/all_gather | solution.py:53
  12.1 332.7 %all-gather.11.cloned.1.call-start = ((), (), s32[]{:S(2)}) async-start(), calls=%async_computation.4 | async-start | bytes 4128768 | tf_op jit(solution)/shard_map/all_gather | solution.py:60
  168.4 2.5 copy-start
  168.4 5.0 %copy-start.2 = (bf16[112,2048]{1,0:T(8,128)(2,1)S(1)}, bf16[112,2048]{1,0:T(8,128)(2,1)}, u32[]{:S(2)}) copy-start(bf16[112,2048]{1,0:T(8,128)(2,1)} %param.10) | copy-start | bytes 1376260
  168.5 5.0 %copy-start.3 = (s32[112,64]{0,1:T(8,128)S(1)}, s32[112,64]{0,1:T(8,128)}, u32[]{:S(2)}) copy-start(s32[112,64]{0,1:T(8,128)} %param.13) | copy-start | bytes 86020
  170.9 82.4 %collective-permute-start = (f32[2,512,896]{1,2,0:T(8,128)}, f32[2,512,896]{1,2,0:T(8,128)}, u32[]{:S(2)}, u32[]{:S(2)}) collective-permute-start(f32[2,512,896]{1,2,0:T(8,128)} %pad_maximum_fusion), channel_id=1, source_target_pairs={{0,1},{1,0},{2,3},{3,2},{4,5},{5,4},{6,7},{7,6},{8,9},{9,8},{10,11... | collective-permute-start | bytes 11010056 | tf_op jit(solution)/shard_map/ppermute | solution.py:58
  175.0 242.9 %reduce-scatter.2.cloned.1.call-start = ((), (), s32[]{:S(2)}) async-start(), calls=%async_computation.5 | async-start | bytes 4456448 | tf_op jit(solution)/shard_map/reduce_scatter | solution.py:61
  175.0 164.5 %copy-start.1 = (f32[1,512,896]{1,2,0:T(8,128)S(1)}, f32[1,512,896]{1,2,0:T(8,128)}, u32[]{:S(2)}) copy-start(f32[1,512,896]{1,2,0:T(8,128)} %copy-done) | copy-start | bytes 5505028
  256.8 82.7 %collective-permute-start.1 = (f32[2,512,896]{1,2,0:T(8,128)S(1)}, f32[2,512,896]{1,2,0:T(8,128)S(1)}, u32[]{:S(2)}, u32[]{:S(2)}) collective-permute-start(f32[2,512,896]{1,2,0:T(8,128)S(1)} %fusion.35), channel_id=1, source_target_pairs={{0,2},{1,3},{2,0},{3,1},{4,6},{5,7},{6,4},{7,5},{8,10},{9,11},{10,... | collective-permute-start | bytes 11010056 | tf_op jit(solution)/shard_map/ppermute | solution.py:58
Sparse Core Ops, SparseCore 0:
  9.5 46.3 all-gather.6
  57.9 52.1 all-gather.8
  112.2 51.4 all-gather.4
  175.1 51.9 all-gather.10
  352.5 65.3 reduce-scatter.1
